TPU v7x, 128 devices: a whole 4x4x4 slice. The times are simulated.
128 devices in a mesh: shard: 32 (over y, z, core), split: 4 (over x).
Axes of the slice: x: 4, y: 4, z: 4, core: 2. Of those that a mesh axis runs over, the one named last changes fastest.
Arguments:
- embeddings: bfloat16 [16384, 1024], P(('shard', 'split')), may hold values from -6 to 6
- order_rank: int32 [16384], P(('shard', 'split')), may hold values from 0 to 16383, each once
- labels: int32 [16384], P(('shard', 'split')), may hold values from 0 to 23
- send_list: int32 [128, 32, 8], P(('shard', 'split')), may hold values from -1 to 127, as said below
Outputs:
- dup_score: float32 [16384], P(('shard', 'split'))
Inputs may be any that keep to these rules, and one draw needn't show every extreme that they name: send_list[d, o, j] is a local row index of device d, or -1 for an empty slot; in each list the filled slots come first; every local row stands in exactly one slot of its device; in every draw one owner shard receives 8 rows from every device.
All inputs are finite; a program needn't handle non-finite values.
Results may differ from a plain program's by a relative error of at most 0.00056.
Values may be sent and summed in bfloat16 or wider, within the bound.
A program may use at most 64 MiB of HBM per device.

v0:
```python
import jax
import jax.numpy as jnp
from jax import lax
from jax.sharding import PartitionSpec as P

OWN_CLUSTERS = 24


def make_fold(queries, query_cluster, query_rank):

    def fold(best, piece, start):
        keys, key_cluster, key_rank = piece
        count = keys.shape[0]
        width = 512
        blocks = count // width
        stacked = (
            keys.reshape(blocks, width, keys.shape[1]),
            key_cluster.reshape(blocks, width),
            key_rank.reshape(blocks, width),
        )

        def step(carry, block):
            block_keys, block_cluster, block_rank = block
            scores = lax.dot_general(
                queries, block_keys, (((1,), (1,)), ((), ())), preferred_element_type=jnp.float32
            )
            match = (
                (query_cluster[:, None] == block_cluster[None, :])
                & (block_cluster[None, :] >= 0)
                & (block_rank[None, :] < query_rank[:, None])
            )
            return (jnp.maximum(carry, jnp.max(jnp.where(match, scores, -1.0), axis=1)), None)

        result, unused = lax.scan(step, best, stacked)
        return result

    return fold


def local(embeddings, order_rank, labels, send_list):
    n_shard = lax.axis_size("shard")
    n_split = lax.axis_size("split")
    slots = send_list[0]
    capacity = slots.shape[1]
    rows_dev = embeddings.shape[0]
    width = embeddings.shape[1]
    floats = embeddings.astype(jnp.float32)
    normed = (floats * lax.rsqrt(jnp.sum(floats * floats, axis=1, keepdims=True) + 1e-06)).astype(
        jnp.bfloat16
    )
    valid_slot = slots >= 0
    safe_slot = jnp.where(valid_slot, slots, 0)
    outgoing = jnp.take(normed, safe_slot.reshape(-1), axis=0).reshape(n_shard, capacity, width)
    owner_ids = lax.broadcasted_iota(jnp.int32, slots.shape, 0)
    cluster = jnp.where(valid_slot, owner_ids * OWN_CLUSTERS + jnp.take(labels, safe_slot), -1)
    rank_out = jnp.take(order_rank, safe_slot)

    def replicate(array):
        wide = jnp.broadcast_to(array[:, None], (n_shard, n_split) + array.shape[1:])
        return wide.reshape((n_shard * n_split,) + array.shape[1:])

    got_rows, got_cluster, got_rank = (
        lax.all_to_all(
            replicate(outgoing), ("shard", "split"), split_axis=0, concat_axis=0, tiled=True
        ),
        lax.all_to_all(
            replicate(cluster), ("shard", "split"), split_axis=0, concat_axis=0, tiled=True
        ),
        lax.all_to_all(
            replicate(rank_out), ("shard", "split"), split_axis=0, concat_axis=0, tiled=True
        ),
    )
    mine = lax.axis_index("split")

    def own_part(array):
        grouped = array.reshape((n_shard, n_split) + array.shape[1:])
        picked = lax.dynamic_index_in_dim(grouped, mine, 1, keepdims=False)
        return picked.reshape((n_shard * capacity,) + array.shape[2:])

    queries = own_part(got_rows)
    query_cluster = own_part(got_cluster)
    query_rank = own_part(got_rank)
    every = n_shard * n_split * capacity
    fold = make_fold(queries, query_cluster, query_rank)
    start_best = jnp.full((n_shard * capacity,), -1.0, jnp.float32)
    best = fold(
        start_best,
        (got_rows.reshape(every, width), got_cluster.reshape(every), got_rank.reshape(every)),
        0,
    )
    returned = lax.all_to_all(
        best.reshape(n_shard, capacity), "shard", split_axis=0, concat_axis=0, tiled=True
    )
    target = jnp.where(valid_slot, slots, rows_dev).reshape(-1)
    return jnp.zeros((rows_dev,), jnp.float32).at[target].set(returned.reshape(-1), mode="drop")


def solution(mesh):
    return jax.shard_map(
        local,
        mesh=mesh,
        in_specs=(
            P(("shard", "split"), None),
            P(("shard", "split")),
            P(("shard", "split")),
            P(("shard", "split"), None, None),
        ),
        out_specs=P(("shard", "split")),
        check_vma=False,
    )
```

profile of v0, /device:TPU:1, one launch (start us, length us, event | category | flops | bytes accessed | tf_op | source)
XLA Modules:
  0.0 93.4 jit_solution(5050868517010825570)
XLA Ops:
  0.0 0.8 copy.12
  0.8 0.1 reshape.165
  0.9 1.9 %gather_fusion.2 = s32[256]{0:T(256)S(1)} fusion(s32[128]{0:T(128)S(1)} %copy-done, s32[1024]{0:T(1024)S(1)} %pad_clamp_fusion.1), kind=kCustom, calls=%fused_computation.1.clone | custom fusion | bytes 3072 | tf_op jit(solution)/shard_map/jit(_take)/gather | solution.py:56
  2.9 0.5 copy-done.1
  3.4 1.9 %gather_fusion.1 = s32[256]{0:T(256)S(1)} fusion(s32[128]{0:T(128)S(1)} %copy-done.1, s32[1024]{0:T(1024)S(1)} %pad_clamp_fusion.1), kind=kCustom, calls=%fused_computation.clone | custom fusion | bytes 3072 | tf_op jit(solution)/shard_map/jit(_take)/gather | solution.py:55
  5.5 0.6 broadcast_in_dim.60
  6.1 11.5 %all-to-all-start = ((s32[128,1,8]{2,1,0:T(1,128)}), s32[128,1,8]{2,1,0:T(1,128)S(1)}, u32[]{:S(2)}, u32[]{:S(2)}) async-start(s32[128,1,8]{2,1,0:T(1,128)} %bitcast.2), calls=%async_computation | async-start | bytes 131072 | tf_op jit(solution)/shard_map/all_to_all | solution.py:66
  17.7 0.1 fusion.5
  17.9 0.1 fusion.6
  18.0 1.2 %gather_fusion = bf16[256,1024]{1,0:T(8,128)(2,1)S(1)} fusion(bf16[128,1024]{1,0:T(8,128)(2,1)S(1)} %fusion.6, s32[1024]{0:T(1024)S(1)} %pad_clamp_fusion), kind=kCustom, calls=%fused_computation.2 | custom fusion | bytes 1049600 | tf_op jit(solution)/shard_map/jit(_take)/gather | solution.py:53
  19.2 8.3 %all-to-all-done = s32[128,1,8]{2,1,0:T(1,128)S(1)} async-done(((s32[128,1,8]{2,1,0:T(1,128)}), s32[128,1,8]{2,1,0:T(1,128)S(1)}, u32[]{:S(2)}, u32[]{:S(2)}) %all-to-all-start) | async-done | bytes 4128 | tf_op jit(solution)/shard_map/all_to_all | solution.py:66
  27.5 0.6 broadcast_in_dim.61
  28.1 4.0 %all-to-all-start.1 = ((s32[128,1,8]{2,1,0:T(1,128)}), s32[128,1,8]{2,1,0:T(1,128)S(1)}, u32[]{:S(2)}, u32[]{:S(2)}) async-start(s32[128,1,8]{2,1,0:T(1,128)} %bitcast.5), calls=%async_computation.1 | async-start | bytes 131072 | tf_op jit(solution)/shard_map/all_to_all | solution.py:69
  32.2 0.1 bitcast_select_fusion
  32.3 9.8 %all-to-all-done.1 = s32[128,1,8]{2,1,0:T(1,128)S(1)} async-done(((s32[128,1,8]{2,1,0:T(1,128)}), s32[128,1,8]{2,1,0:T(1,128)S(1)}, u32[]{:S(2)}, u32[]{:S(2)}) %all-to-all-start.1) | async-done | bytes 4128 | tf_op jit(solution)/shard_map/all_to_all | solution.py:69
  42.1 1.6 %broadcast_in_dim.64 = bf16[32,4,8,1024]{3,2,1,0:T(8,128)(2,1)} broadcast(bf16[32,8,1024]{2,1,0:T(8,128)(2,1)S(1)} %bitcast_select_fusion), dimensions={0,2,3} | broadcast | bytes 2621440 | tf_op jit(solution)/shard_map/broadcast_in_dim | solution.py:59
  43.7 4.0 %all-to-all-start.2 = ((bf16[128,8,1024]{2,1,0:T(8,128)(2,1)}), bf16[128,8,1024]{2,1,0:T(8,128)(2,1)S(1)}, u32[]{:S(2)}, u32[]{:S(2)}) async-start(bf16[128,8,1024]{2,1,0:T(8,128)(2,1)} %bitcast.10), calls=%async_computation.2 | async-start | bytes 4194304 | tf_op jit(solution)/shard_map/all_to_all | solution.py:63
  47.8 0.5 broadcast.129
  48.3 0.8 reduce.11
  49.1 0.1 reshape_reshape.9
  49.2 0.8 reduce.12
  49.9 0.1 reshape_reshape.10
  50.2 0.1 eq.25
  50.3 28.4 %all-to-all-done.2 = bf16[128,8,1024]{2,1,0:T(8,128)(2,1)S(1)} async-done(((bf16[128,8,1024]{2,1,0:T(8,128)(2,1)}), bf16[128,8,1024]{2,1,0:T(8,128)(2,1)S(1)}, u32[]{:S(2)}, u32[]{:S(2)}) %all-to-all-start.2) | async-done | bytes 2097184 | tf_op jit(solution)/shard_map/all_to_all | solution.py:63
  78.8 1.2 %while.12 = (s32[]{:T(128)}, f32[256]{0:T(256)S(1)}, s32[32,8]{1,0:T(8,128)}, s32[2,512]{1,0:T(2,128)S(1)}, s32[2,512]{1,0:T(2,128)S(1)}, /*index=5*/s32[32,8]{1...) while((s32[]{:T(128)}, f32[256]{0:T(256)S(1)}, ...), condition=%wide.wide.region_3.5_spmd.clone, body=%wide.wide.region_1.0_spmd.clone.sunk | while | flops 269222656 | bytes 1592467 | solution.py:34
  78.9 0.5 fusion.18
  79.4 0.5 fusion.18
  80.1 10.1 %all_to_all.32 = f32[32,1,8]{2,1,0:T(1,128)S(1)} all-to-all(f32[32,1,8]{2,1,0:T(1,128)S(1)} %bitcast.57), channel_id=1, replica_groups=mesh['shard'=32,'split'=4] {'shard'}, dimensions={0} | all-to-all | bytes 2048 | tf_op jit(solution)/shard_map/all_to_all | solution.py:91
  90.2 0.5 broadcast.131
  90.7 0.7 reduce.13
  91.4 0.1 reshape.157
  91.5 1.9 %scatter_custom_fusion = f32[128]{0:T(128)} fusion(s32[256]{0:T(256)S(1)} %bitcast.61, f32[256]{0:T(256)S(1)} %reshape.157, f32[]{:T(128)} %constant.37.clone.1), kind=kCustom, calls=%fused_computation.36 | custom fusion | bytes 516 | tf_op jit(solution)/shard_map/scatter | solution.py:95
  (32 shorter events, 0.7 us)
Async XLA Ops:
  0.0 0.9 copy-start
  2.8 0.7 copy-start.1
  3.4 14.3 %copy-start.2 = (bf16[128,1024]{1,0:T(8,128)(2,1)S(1)}, bf16[128,1024]{1,0:T(8,128)(2,1)}, u32[]{:S(2)}) copy-start(bf16[128,1024]{1,0:T(8,128)(2,1)} %param.8) | copy-start | bytes 786436
  6.1 21.4 %all-to-all-start = ((s32[128,1,8]{2,1,0:T(1,128)}), s32[128,1,8]{2,1,0:T(1,128)S(1)}, u32[]{:S(2)}, u32[]{:S(2)}) async-start(s32[128,1,8]{2,1,0:T(1,128)} %bitcast.2), calls=%async_computation | async-start | bytes 131072 | tf_op jit(solution)/shard_map/all_to_all | solution.py:66
  28.1 13.9 %all-to-all-start.1 = ((s32[128,1,8]{2,1,0:T(1,128)}), s32[128,1,8]{2,1,0:T(1,128)S(1)}, u32[]{:S(2)}, u32[]{:S(2)}) async-start(s32[128,1,8]{2,1,0:T(1,128)} %bitcast.5), calls=%async_computation.1 | async-start | bytes 131072 | tf_op jit(solution)/shard_map/all_to_all | solution.py:69
  43.7 35.0 %all-to-all-start.2 = ((bf16[128,8,1024]{2,1,0:T(8,128)(2,1)}), bf16[128,8,1024]{2,1,0:T(8,128)(2,1)S(1)}, u32[]{:S(2)}, u32[]{:S(2)}) async-start(bf16[128,8,1024]{2,1,0:T(8,128)(2,1)} %bitcast.10), calls=%async_computation.2 | async-start | bytes 4194304 | tf_op jit(solution)/shard_map/all_to_all | solution.py:63
  50.1 28.7 %copy-start.3 = (s32[32,1,8]{2,1,0:T(1,128)}, s32[32,1,8]{2,1,0:T(1,128)S(1)}, u32[]{:S(2)}) copy-start(s32[32,1,8]{2,1,0:T(1,128)S(1)} %constant_dynamic-slice_fusion.2) | copy-start | bytes 3076
  50.2 28.6 %copy-start.4 = (s32[32,1,8]{2,1,0:T(1,128)}, s32[32,1,8]{2,1,0:T(1,128)S(1)}, u32[]{:S(2)}) copy-start(s32[32,1,8]{2,1,0:T(1,128)S(1)} %constant_dynamic-slice_fusion.3) | copy-start | bytes 3076
where the time goes:
time: 93.7 us; the launch traced here: 93.4 us
  waiting for transfers between devices  46.5 us (50%)
  starting transfers between devices  19.6 us (21%)
  local copies, waits for them, and re-layouts  13 us (14%)
  blocking collectives  10.1 us (11%)
  other arithmetic  2.83 us (3%)
  matrix products  1 us (1%)
    all_to_all x1, waiting for transfers between devices, local(): lax.all_to_all(replicate(outgoing), ('shard', 'split'), split_axis=0, con...  28.4 us
    all_to_all x1, starting transfers between devices, local(): lax.all_to_all(replicate(cluster), ('shard', 'split'), split_axis=0, conc...  11.5 us
    all_to_all x1, blocking collectives, local(): lax.all_to_all(best.reshape(n_shard, capacity), 'shard', split_axis=0, co...  10.1 us
    all_to_all x1, waiting for transfers between devices, local(): lax.all_to_all(replicate(rank_out), ('shard', 'split'), split_axis=0, con...  9.77 us
    all_to_all x1, waiting for transfers between devices, local(): lax.all_to_all(replicate(cluster), ('shard', 'split'), split_axis=0, conc...  8.33 us
    all_to_all x1, starting transfers between devices, local(): lax.all_to_all(replicate(outgoing), ('shard', 'split'), split_axis=0, con...  4.05 us
    all_to_all x1, starting transfers between devices, local(): lax.all_to_all(replicate(rank_out), ('shard', 'split'), split_axis=0, con...  4.05 us
    broadcast_in_dim x3, local copies, waits for them, and re-layouts, replicate(): jnp.broadcast_to(array[:, None], (n_shard, n_split) + array.shape[1:])  2.89 us
  transfers between devices with their start and end apart: 3, of which 3 were waited for; matrix products, arithmetic and copies ran while one was open for 4% of the time, Pallas kernels for 0%

commit v1 on v0

v1 whole, which is shorter than its diff:
```python
import jax
import jax.numpy as jnp
from jax import lax
from jax.experimental import pallas as pl
from jax.experimental.pallas import tpu as pltpu
from jax.sharding import PartitionSpec as P

N_SHARD = 32
N_SPLIT = 4
DEVICES = N_SHARD * N_SPLIT
CAP = 8
GROUPS = 4
LANES = 128
RANK_SPAN = 16384
MESH = pl.DeviceIdType.MESH


def home(owner):
    return (owner >> 3) * 8 + ((owner >> 2) & 1) * 2 + 1, owner & 3


def place_of(y, z, core, x):
    kind = jnp.where(z < 2, z * 2 + core, 6 - core * 2 + (z & 1))
    return kind * 16 + y * 4 + x


def source(place):
    kind = place >> 4
    low = kind < 4
    z = jnp.where(low, kind >> 1, 2 + (kind & 1))
    core = jnp.where(low, kind & 1, 1 - ((kind >> 1) & 1))
    return ((place >> 2) & 3) * 8 + z * 2 + core, place & 3


def iota(shape, axis):
    return lax.broadcasted_iota(jnp.int32, shape, axis)


def wait_bytes(ref, sem):
    pltpu.make_async_copy(ref, ref, sem).wait()


def slot_masks(lists):
    slots = N_SHARD * CAP
    pick = (iota((slots, CAP), 0) % CAP == iota((slots, CAP), 1)).astype(jnp.bfloat16)
    spread = jnp.dot(pick, lists.astype(jnp.float32).astype(jnp.bfloat16), preferred_element_type=jnp.float32)
    mine = iota((slots, N_SHARD), 0) // CAP == iota((slots, N_SHARD), 1)
    slot = jnp.sum(jnp.where(mine, spread, 0.0), axis=1, keepdims=True)
    return slot == iota((slots, LANES), 1).astype(jnp.float32)


def fill_codes(chosen, labels, ranks, outgoing_code):
    code = ((labels + 1) * RANK_SPAN + ranks).astype(jnp.float32)
    code = jnp.sum(jnp.where(chosen, code, 0.0), axis=1, keepdims=True).reshape(N_SHARD, CAP, 1)
    diagonal = iota((N_SHARD, CAP, LANES), 1) == iota((N_SHARD, CAP, LANES), 2)
    outgoing_code[...] = jnp.sum(jnp.where(diagonal, code, 0.0), axis=1, keepdims=True)


def fill_rows(chosen, embeddings, outgoing):
    floats = embeddings.astype(jnp.float32)
    normed = (floats * lax.rsqrt(jnp.sum(floats * floats, axis=1, keepdims=True) + 1e-06)).astype(jnp.bfloat16)
    picked = jnp.dot(chosen.astype(jnp.bfloat16), normed, preferred_element_type=jnp.float32)
    outgoing[...] = picked.astype(jnp.bfloat16).reshape(outgoing.shape)


def kernel(
    emb_hbm,
    rank_hbm,
    label_hbm,
    list_hbm,
    out_ref,
    emb_ref,
    rank_ref,
    label_ref,
    list_ref,
    relay_emb,
    relay_rank,
    relay_label,
    relay_list,
    outgoing,
    outgoing_code,
    relay_outgoing,
    relay_outgoing_code,
    rows,
    codes,
    table,
    code_col,
    best,
    returned,
    in_sem,
    relay_send_sem,
    relay_recv_sem,
    send_sem,
    send_code_sem,
    relay_out_sem,
    relay_out_code_sem,
    recv_sem,
    recv_code_sem,
    back_send_sem,
    back_recv_sem,
):
    shard = lax.axis_index("shard")
    split = lax.axis_index("split")
    y, z, core = shard >> 3, (shard >> 1) & 3, shard & 1
    width = emb_ref.shape[1]
    per_group = DEVICES // GROUPS
    low = z < 2
    is_home = jnp.logical_and(core == 1, low)
    is_relay = jnp.logical_and(core == 0, low)
    is_relayed = jnp.logical_and(core == 0, jnp.logical_not(low))
    is_direct = jnp.logical_not(is_relayed)
    opposite = shard + (3 - 2 * z) * 2
    own = y * 8 + (z & 1) * 4 + split
    own_place = place_of(y, z, core, split)

    barrier = pltpu.get_barrier_semaphore()

    @pl.when(is_home)
    def _():
        def greet(place):
            pl.semaphore_signal(barrier, inc=1, device_id=source(place), device_id_type=MESH)

        def greet_high(i, carry):
            greet(64 + ((own_place + i) & 31))
            return carry

        def greet_low(i, carry):
            greet((own_place + i) & 63)
            return carry

        lax.fori_loop(0, 32, greet_high, 0)
        lax.fori_loop(1, 64, greet_low, 0)

    @pl.when(is_relay)
    def _():
        pl.semaphore_signal(barrier, inc=1, device_id=(opposite, split), device_id_type=MESH)

    inputs = (list_hbm, rank_hbm, label_hbm, emb_hbm)
    relayed = (relay_list, relay_rank, relay_label, relay_emb)

    def relay_copy(i):
        return pltpu.make_async_remote_copy(
            src_ref=inputs[i],
            dst_ref=relayed[i],
            send_sem=relay_send_sem.at[i],
            recv_sem=relay_recv_sem.at[i],
            device_id=(opposite, split),
            device_id_type=MESH,
        )

    @pl.when(is_relayed)
    def _():
        pl.semaphore_wait(barrier, 1)
        for i in range(4):
            relay_copy(i).start()
        for i in range(4):
            relay_copy(i).wait_send()
        pl.semaphore_signal(barrier, inc=1, device_id=(shard + 1, split), device_id_type=MESH)

    loads = [
        pltpu.make_async_copy(src, dst, in_sem.at[i])
        for i, (src, dst) in enumerate(zip(inputs, (list_ref, rank_ref, label_ref, emb_ref)))
    ]
    for load in loads:
        load.start()
    for load in loads[:3]:
        load.wait()
    chosen = slot_masks(list_ref[...])
    loads[3].wait()

    def send(i, place, code_ref, code_sem, row_ref, row_sem):
        owner = (own + i) & (N_SHARD - 1)
        for src, dst, sem, arrived in ((code_ref, codes, code_sem, recv_code_sem), (row_ref, rows, row_sem, recv_sem)):
            pltpu.make_async_remote_copy(
                src_ref=src.at[owner],
                dst_ref=dst.at[place],
                send_sem=sem,
                recv_sem=arrived.at[place >> 5],
                device_id=home(owner),
                device_id_type=MESH,
            ).start()

    @pl.when(is_direct)
    def _():
        fill_codes(chosen, label_ref[...], rank_ref[...], outgoing_code)
        fill_rows(chosen, emb_ref[...], outgoing)
        pl.semaphore_wait(barrier, jnp.where(is_home, N_SHARD - 1, jnp.where(low, N_SHARD, N_SHARD + 1)))

        def send_own(i, carry):
            send(i, own_place, outgoing_code, send_code_sem, outgoing, send_sem)
            return carry

        @pl.when(is_home)
        def _():
            group = own_place >> 5
            pltpu.make_async_copy(outgoing_code.at[own], codes.at[own_place], recv_code_sem.at[group]).start()
            pltpu.make_async_copy(outgoing.at[own], rows.at[own_place], recv_sem.at[group]).start()

        @pl.when(jnp.logical_not(is_home))
        def _():
            send_own(0, 0)

        lax.fori_loop(1, N_SHARD, send_own, 0)

    @pl.when(is_relay)
    def _():
        for i in range(4):
            relay_copy(i).wait_recv()
        relay_chosen = slot_masks(relay_list[...])
        fill_codes(relay_chosen, relay_label[...], relay_rank[...], relay_outgoing_code)
        fill_rows(relay_chosen, relay_emb[...], relay_outgoing)
        place = place_of(y, 3 - z, core, split)

        def send_relayed(i, carry):
            send(i, place, relay_outgoing_code, relay_out_code_sem, relay_outgoing, relay_out_sem)
            return carry

        lax.fori_loop(0, N_SHARD, send_relayed, 0)

    @pl.when(is_home)
    def _():
        contract = (((1,), (1,)), ((), ()))
        size = per_group * CAP
        tiles = size // LANES
        square = iota((LANES, LANES), 0) == iota((LANES, LANES), 1)
        diagonal = iota((per_group, CAP, LANES), 1) == iota((per_group, CAP, LANES), 2)
        uppers, lowers, bests = [], [], []

        def scored(scores, tile, col, query):
            match = (col < uppers[query]) & (col >= lowers[query])
            scores = scores[:, tile * LANES : (tile + 1) * LANES]
            return jnp.max(jnp.where(match, scores, -1.0), axis=0, keepdims=True)

        for g in range(GROUPS):
            part = pl.ds(g * per_group, per_group)
            here = pl.ds(g * size, size)
            wait_bytes(codes.at[part], recv_code_sem.at[g])
            col = jnp.sum(jnp.where(diagonal, codes[part], 0.0), axis=2, keepdims=True).reshape(size, 1)
            col = jnp.broadcast_to(col, (size, LANES))
            code_col[here] = col
            for t in range(tiles):
                upper = jnp.sum(jnp.where(square, col[t * LANES : (t + 1) * LANES], 0.0), axis=0, keepdims=True)
                uppers.append(upper)
                lowers.append(jnp.floor(upper * (1.0 / RANK_SPAN)) * RANK_SPAN)

            wait_bytes(rows.at[part], recv_sem.at[g])
            fresh = rows[part].reshape(size, width)
            table[here] = fresh
            upto = (g + 1) * size
            scores = lax.dot_general(table[:upto], fresh, contract, preferred_element_type=jnp.float32)
            for t in range(tiles):
                bests.append(scored(scores, t, code_col[:upto], g * tiles + t))
            if g:
                scores = lax.dot_general(fresh, table[: g * size], contract, preferred_element_type=jnp.float32)
                for q in range(g * tiles):
                    bests[q] = jnp.maximum(bests[q], scored(scores, q, col, q))
        for q in range(GROUPS * tiles):
            best[q] = bests[q]

        pltpu.make_async_copy(best.at[own_place >> 4], returned.at[own], back_recv_sem).start()

        def back(place, carry):
            @pl.when(place != own_place)
            def _():
                pltpu.make_async_remote_copy(
                    src_ref=best.at[place >> 4],
                    dst_ref=returned.at[own],
                    send_sem=back_send_sem,
                    recv_sem=back_recv_sem,
                    device_id=source(place),
                    device_id_type=MESH,
                ).start()

            return carry

        lax.fori_loop(0, DEVICES, back, 0)

    lane = (y * 4 + split) * CAP + iota((N_SHARD, CAP, LANES), 1)
    there = iota((N_SHARD, CAP, LANES), 2) == lane
    wait_bytes(returned, back_recv_sem)
    value = jnp.sum(jnp.where(there, returned[...], 0.0), axis=2, keepdims=True)
    result = jnp.where(chosen, value.reshape(N_SHARD * CAP, 1), 0.0)
    out_ref[...] = jnp.sum(result.reshape(N_SHARD, CAP, LANES), axis=0)

    @pl.when(is_home)
    def _():
        wait_bytes(outgoing.at[pl.ds(0, N_SHARD - 1)], send_sem)
        wait_bytes(outgoing_code.at[pl.ds(0, N_SHARD - 1)], send_code_sem)
        wait_bytes(codes.at[pl.ds(0, DEVICES - 1)], back_send_sem)

    @pl.when(jnp.logical_and(is_direct, jnp.logical_not(is_home)))
    def _():
        wait_bytes(outgoing, send_sem)
        wait_bytes(outgoing_code, send_code_sem)

    @pl.when(is_relay)
    def _():
        wait_bytes(relay_outgoing, relay_out_sem)
        wait_bytes(relay_outgoing_code, relay_out_code_sem)

def local(embeddings, order_rank, labels, send_list):
    rows_dev, width = embeddings.shape
    in_hbm = pl.BlockSpec(memory_space=pltpu.MemorySpace.HBM)
    result = pl.pallas_call(
        kernel,
        out_shape=jax.ShapeDtypeStruct((8, rows_dev), jnp.float32),
        in_specs=[in_hbm] * 4,
        out_specs=pl.BlockSpec(memory_space=pltpu.VMEM),
        scratch_shapes=[
            pltpu.VMEM((rows_dev, width), jnp.bfloat16),
            pltpu.VMEM((1, rows_dev), jnp.int32),
            pltpu.VMEM((1, rows_dev), jnp.int32),
            pltpu.VMEM((CAP, N_SHARD), jnp.int32),
            pltpu.VMEM((rows_dev, width), jnp.bfloat16),
            pltpu.VMEM((1, rows_dev), jnp.int32),
            pltpu.VMEM((1, rows_dev), jnp.int32),
            pltpu.VMEM((CAP, N_SHARD), jnp.int32),
            pltpu.VMEM((N_SHARD, CAP, width), jnp.bfloat16),
            pltpu.VMEM((N_SHARD, 1, LANES), jnp.float32),
            pltpu.VMEM((N_SHARD, CAP, width), jnp.bfloat16),
            pltpu.VMEM((N_SHARD, 1, LANES), jnp.float32),
            pltpu.VMEM((DEVICES, CAP, width), jnp.bfloat16),
            pltpu.VMEM((DEVICES, 1, LANES), jnp.float32),
            pltpu.VMEM((DEVICES * CAP, width), jnp.bfloat16),
            pltpu.VMEM((DEVICES * CAP, LANES), jnp.float32),
            pltpu.VMEM((DEVICES * CAP // LANES, 1, LANES), jnp.float32),
            pltpu.VMEM((N_SHARD, 1, LANES), jnp.float32),
            pltpu.SemaphoreType.DMA((4,)),
            pltpu.SemaphoreType.DMA((4,)),
            pltpu.SemaphoreType.DMA((4,)),
            pltpu.SemaphoreType.DMA,
            pltpu.SemaphoreType.DMA,
            pltpu.SemaphoreType.DMA,
            pltpu.SemaphoreType.DMA,
            pltpu.SemaphoreType.DMA((GROUPS,)),
            pltpu.SemaphoreType.DMA((GROUPS,)),
            pltpu.SemaphoreType.DMA,
            pltpu.SemaphoreType.DMA,
        ],
        compiler_params=pltpu.CompilerParams(
            collective_id=0, has_side_effects=True, vmem_limit_bytes=64 * 1024 * 1024
        ),
    )(embeddings, order_rank.reshape(1, rows_dev), labels.reshape(1, rows_dev), send_list[0].T)
    return jnp.sum(result, axis=0)


def solution(mesh):
    return jax.shard_map(
        local,
        mesh=mesh,
        in_specs=(
            P(("shard", "split"), None),
            P(("shard", "split")),
            P(("shard", "split")),
            P(("shard", "split"), None, None),
        ),
        out_specs=P(("shard", "split")),
        check_vma=False,
    )
```

time: 93.7 us -> 29.3 us (0.31)
  waiting for transfers between devices: 46.5 us -> 0 us
  Pallas kernels: 0 us -> 27.9 us
  starting transfers between devices: 19.6 us -> 0 us
  local copies, waits for them, and re-layouts: 13 us -> 0 us
  blocking collectives: 10.1 us -> 0 us
  other arithmetic: 2.83 us -> 1.21 us
  matrix products: 1 us -> 0 us
    all_to_all x3 -> x0, waiting for transfers between devices: 46.5 us -> none  [the longest x1 28.4 us: local(): lax.all_to_all(replicate(outgoing), ('shard', 'split'), split_axis=0, con...]
    pallas_call x0 -> x1, Pallas kernels: none -> 27.9 us  [local(): pl.pallas_call(kernel, out_shape=jax.ShapeDtypeStruct((8, rows_dev), jnp....]
    all_to_all x3 -> x0, starting transfers between devices: 19.6 us -> none  [the longest x1 11.5 us: local(): lax.all_to_all(replicate(cluster), ('shard', 'split'), split_axis=0, conc...]
    all_to_all x1 -> x0, blocking collectives: 10.1 us -> none  [local(): lax.all_to_all(best.reshape(n_shard, capacity), 'shard', split_axis=0, co...]
    gather x5 -> x0, local copies, waits for them, and re-layouts: 5.06 us -> none  [the longest x2 1.95 us: local(): rank_out = jnp.take(order_rank, safe_slot)]
    broadcast_in_dim x4 -> x0, local copies, waits for them, and re-layouts: 2.97 us -> none  [the longest x3 2.89 us: replicate(): jnp.broadcast_to(array[:, None], (n_shard, n_split) + array.shape[1:])]
    all_to_all x3 -> x0, other arithmetic: 2.24 us -> none  [the longest x1 0.78 us: local(): lax.all_to_all(replicate(rank_out), ('shard', 'split'), split_axis=0, con...]
    scatter x1 -> x0, local copies, waits for them, and re-layouts: 1.89 us -> none  [local(): jnp.zeros((rows_dev,), jnp.float32).at[target]]
  transfers between devices with their start and end apart: 3 -> 0, of which waited for: 3 -> 0; matrix products, arithmetic and copies ran while one was open for 4% -> 0% of each run, Pallas kernels for 0% -> 0%
where the time goes in v1:
time: 29.3 us; the launch traced here: 29.1 us
  Pallas kernels  27.9 us (95%)
  other arithmetic  1.21 us (4%)
    pallas_call x1, Pallas kernels, local(): pl.pallas_call(kernel, out_shape=jax.ShapeDtypeStruct((8, rows_dev), jnp....  27.9 us
    reduce_sum x1, other arithmetic, local(): return jnp.sum(result, axis=0)  1.21 us

profile of v1, /device:TPU:1, one launch (start us, length us, event | category | flops | bytes accessed | tf_op | source)
XLA Modules:
  0.0 29.1 jit_solution(5688243631687823903)
XLA Ops:
  0.0 27.9 %shard_map.46 = f32[8,128]{1,0:T(8,128)} custom-call(bf16[128,1024]{1,0:T(8,128)(2,1)} %emb_hbm.1, s32[1,128]{1,0:T(1,128)} %bitcast.6, s32[1,128]{1,0:T(1,128)} %bitcast.7, s32[8,32]{1,0:T(8,128)} %bitcast.5), custom_call_target="tpu_custom_call" | custom-call | tf_op jit(solution)/shard_map/pallas_call | solution.py:304
  27.9 1.2 %reduce_sum.9 = f32[128]{0:T(128)} reduce(f32[8,128]{1,0:T(8,128)} %shard_map.46, f32[]{:T(128)} %constant.0.clone.1), dimensions={0}, to_apply=%region_0.0 | reduce | flops 896 | bytes 4612 | tf_op jit(solution)/shard_map/reduce_sum | solution.py:344

commit v2 on v1

--- a/solution.py
+++ b/solution.py
@@ -17,6 +17,9 @@
 
 def home(owner):
     return (owner >> 3) * 8 + ((owner >> 2) & 1) * 2 + 1, owner & 3
+
+
+KINDS = ((0, 0), (0, 1), (1, 0), (1, 1), (2, 1), (3, 1), (2, 0), (3, 0))
 
 
 def place_of(y, z, core, x):
@@ -128,8 +131,8 @@
             greet((own_place + i) & 63)
             return carry
 
+        lax.fori_loop(1, 64, greet_low, 0)
         lax.fori_loop(0, 32, greet_high, 0)
-        lax.fori_loop(1, 64, greet_low, 0)
 
     @pl.when(is_relay)
     def _():
@@ -259,28 +262,34 @@
 
         pltpu.make_async_copy(best.at[own_place >> 4], returned.at[own], back_recv_sem).start()
 
-        def back(place, carry):
-            @pl.when(place != own_place)
-            def _():
-                pltpu.make_async_remote_copy(
-                    src_ref=best.at[place >> 4],
+        def back(column, carry):
+            for kind, (plane, at_core) in enumerate(KINDS):
+                copy = pltpu.make_async_remote_copy(
+                    src_ref=best.at[kind],
                     dst_ref=returned.at[own],
                     send_sem=back_send_sem,
                     recv_sem=back_recv_sem,
-                    device_id=source(place),
+                    device_id=((column >> 2) * 8 + plane * 2 + at_core, column & 3),
                     device_id_type=MESH,
-                ).start()
-
-            return carry
-
-        lax.fori_loop(0, DEVICES, back, 0)
+                )
+                if at_core == 1 and plane < 2:
+
+                    @pl.when(kind * 16 + column != own_place)
+                    def _():
+                        copy.start()
+
+                else:
+                    copy.start()
+            return carry
+
+        lax.fori_loop(0, N_SHARD * N_SPLIT // len(KINDS), back, 0)
 
     lane = (y * 4 + split) * CAP + iota((N_SHARD, CAP, LANES), 1)
     there = iota((N_SHARD, CAP, LANES), 2) == lane
     wait_bytes(returned, back_recv_sem)
     value = jnp.sum(jnp.where(there, returned[...], 0.0), axis=2, keepdims=True)
     result = jnp.where(chosen, value.reshape(N_SHARD * CAP, 1), 0.0)
-    out_ref[...] = jnp.sum(result.reshape(N_SHARD, CAP, LANES), axis=0)
+    out_ref[...] = jnp.sum(result, axis=0, keepdims=True)
 
     @pl.when(is_home)
     def _():
@@ -300,10 +309,12 @@
 
 def local(embeddings, order_rank, labels, send_list):
     rows_dev, width = embeddings.shape
+    inputs = (embeddings, order_rank.reshape(1, rows_dev), labels.reshape(1, rows_dev), send_list[0].T)
+    inputs = [pltpu.with_memory_space_constraint(array, pltpu.MemorySpace.HBM) for array in inputs]
     in_hbm = pl.BlockSpec(memory_space=pltpu.MemorySpace.HBM)
     result = pl.pallas_call(
         kernel,
-        out_shape=jax.ShapeDtypeStruct((8, rows_dev), jnp.float32),
+        out_shape=jax.ShapeDtypeStruct((1, rows_dev), jnp.float32),
         in_specs=[in_hbm] * 4,
         out_specs=pl.BlockSpec(memory_space=pltpu.VMEM),
         scratch_shapes=[
@@ -338,10 +349,10 @@
             pltpu.SemaphoreType.DMA,
         ],
         compiler_params=pltpu.CompilerParams(
-            collective_id=0, has_side_effects=True, vmem_limit_bytes=64 * 1024 * 1024
+            collective_id=0, has_side_effects=True, vmem_limit_bytes=48 * 1024 * 1024
         ),
-    )(embeddings, order_rank.reshape(1, rows_dev), labels.reshape(1, rows_dev), send_list[0].T)
-    return jnp.sum(result, axis=0)
+    )(*inputs)
+    return result[0]
 
 
 def solution(mesh):

time: 29.3 us -> 27.1 us (0.925)
  Pallas kernels: 27.9 us -> 26.4 us
  other arithmetic: 1.21 us -> 0 us
  local copies, waits for them, and re-layouts: 0 us -> 0.51 us
    pallas_call x1, Pallas kernels: 27.9 us -> 26.4 us  [local(): pl.pallas_call(kernel, out_shape=jax.ShapeDtypeStruct((1, rows_dev), jnp....]
    reduce_sum x1 -> x0, other arithmetic: 1.21 us -> none  [local(): return jnp.sum(result, axis=0)]
    unnamed x0 -> x1, local copies, waits for them, and re-layouts: none -> 0.51 us
where the time goes in v2:
time: 27.1 us; the launch traced here: 26.9 us
  Pallas kernels  26.4 us (97%)
  local copies, waits for them, and re-layouts  0.51 us (2%)
    pallas_call x1, Pallas kernels, local(): pl.pallas_call(kernel, out_shape=jax.ShapeDtypeStruct((1, rows_dev), jnp....  26.4 us

profile of v2, /device:TPU:1, one launch (start us, length us, event | category | flops | bytes accessed | tf_op | source)
XLA Modules:
  0.0 26.9 jit_solution(14838963755602636213)
XLA Ops:
  0.0 26.4 %shard_map.46 = f32[1,128]{1,0:T(1,128)S(1)} custom-call(bf16[128,1024]{1,0:T(8,128)(2,1)} %emb_hbm.1, s32[1,128]{1,0:T(1,128)} %bitcast.8, s32[1,128]{1,0:T(1,128)} %bitcast.9, s32[8,32]{1,0:T(8,128)} %bitcast.7), custom_call_target="tpu_custom_call" | custom-call | tf_op jit(solution)/shard_map/pallas_call | solution.py:315
  26.4 0.5 %copy.6 = f32[128]{0:T(128)} copy(f32[128]{0:T(128)S(1)} %bitcast.6) | data formatting | bytes 1024

commit v3 on v2

--- a/solution.py
+++ b/solution.py
@@ -10,6 +10,7 @@
 DEVICES = N_SHARD * N_SPLIT
 CAP = 8
 GROUPS = 4
+PIECES = 4
 LANES = 128
 RANK_SPAN = 16384
 MESH = pl.DeviceIdType.MESH
@@ -25,14 +26,6 @@
 def place_of(y, z, core, x):
     kind = jnp.where(z < 2, z * 2 + core, 6 - core * 2 + (z & 1))
     return kind * 16 + y * 4 + x
-
-
-def source(place):
-    kind = place >> 4
-    low = kind < 4
-    z = jnp.where(low, kind >> 1, 2 + (kind & 1))
-    core = jnp.where(low, kind & 1, 1 - ((kind >> 1) & 1))
-    return ((place >> 2) & 3) * 8 + z * 2 + core, place & 3
 
 
 def iota(shape, axis):
@@ -59,9 +52,12 @@
     outgoing_code[...] = jnp.sum(jnp.where(diagonal, code, 0.0), axis=1, keepdims=True)
 
 
-def fill_rows(chosen, embeddings, outgoing):
+def normalise(embeddings):
     floats = embeddings.astype(jnp.float32)
-    normed = (floats * lax.rsqrt(jnp.sum(floats * floats, axis=1, keepdims=True) + 1e-06)).astype(jnp.bfloat16)
+    return (floats * lax.rsqrt(jnp.sum(floats * floats, axis=1, keepdims=True) + 1e-06)).astype(jnp.bfloat16)
+
+
+def fill_rows(chosen, normed, outgoing):
     picked = jnp.dot(chosen.astype(jnp.bfloat16), normed, preferred_element_type=jnp.float32)
     outgoing[...] = picked.astype(jnp.bfloat16).reshape(outgoing.shape)
 
@@ -118,33 +114,36 @@
 
     barrier = pltpu.get_barrier_semaphore()
 
+    @pl.when(is_relay)
+    def _():
+        pl.semaphore_signal(barrier, inc=1, device_id=(opposite, split), device_id_type=MESH)
+
     @pl.when(is_home)
     def _():
-        def greet(place):
-            pl.semaphore_signal(barrier, inc=1, device_id=source(place), device_id_type=MESH)
-
-        def greet_high(i, carry):
-            greet(64 + ((own_place + i) & 31))
+        def greet(i, carry):
+            column = (y * 4 + split + i) & 15
+            for plane, at_core in ((0, 0), (1, 0), (0, 1), (1, 1), (2, 1), (3, 1)):
+                target = ((column >> 2) * 8 + plane * 2 + at_core, column & 3)
+
+                @pl.when(jnp.logical_or(i != 0, jnp.logical_or(z != plane, at_core == 0)))
+                def _():
+                    pl.semaphore_signal(barrier, inc=1, device_id=target, device_id_type=MESH)
+
             return carry
 
-        def greet_low(i, carry):
-            greet((own_place + i) & 63)
-            return carry
-
-        lax.fori_loop(1, 64, greet_low, 0)
-        lax.fori_loop(0, 32, greet_high, 0)
-
-    @pl.when(is_relay)
-    def _():
-        pl.semaphore_signal(barrier, inc=1, device_id=(opposite, split), device_id_type=MESH)
+        lax.fori_loop(0, 16, greet, 0)
 
     inputs = (list_hbm, rank_hbm, label_hbm, emb_hbm)
-    relayed = (relay_list, relay_rank, relay_label, relay_emb)
+    piece = emb_ref.shape[0] // PIECES
 
     def relay_copy(i):
+        src, dst = (list_hbm, rank_hbm, label_hbm)[i : i + 1], (relay_list, relay_rank, relay_label)[i : i + 1]
+        if i >= 3:
+            part = pl.ds((i - 3) * piece, piece)
+            src, dst = (emb_hbm.at[part],), (relay_emb.at[part],)
         return pltpu.make_async_remote_copy(
-            src_ref=inputs[i],
-            dst_ref=relayed[i],
+            src_ref=src[0],
+            dst_ref=dst[0],
             send_sem=relay_send_sem.at[i],
             recv_sem=relay_recv_sem.at[i],
             device_id=(opposite, split),
@@ -154,11 +153,8 @@
     @pl.when(is_relayed)
     def _():
         pl.semaphore_wait(barrier, 1)
-        for i in range(4):
+        for i in range(3 + PIECES):
             relay_copy(i).start()
-        for i in range(4):
-            relay_copy(i).wait_send()
-        pl.semaphore_signal(barrier, inc=1, device_id=(shard + 1, split), device_id_type=MESH)
 
     loads = [
         pltpu.make_async_copy(src, dst, in_sem.at[i])
@@ -166,13 +162,22 @@
     ]
     for load in loads:
         load.start()
+
+    @pl.when(is_relayed)
+    def _():
+        for i in range(3 + PIECES):
+            relay_copy(i).wait_send()
+        pl.semaphore_signal(barrier, inc=1, device_id=(shard + 1, split), device_id_type=MESH)
+
     for load in loads[:3]:
         load.wait()
     chosen = slot_masks(list_ref[...])
     loads[3].wait()
 
     def send(i, place, code_ref, code_sem, row_ref, row_sem):
-        owner = (own + i) & (N_SHARD - 1)
+        k = i & 15
+        offset = (jnp.where(k < 8, 1479272810, 205723615) >> ((k & 7) * 4)) & 15
+        owner = ((y + (offset >> 2)) & 3) * 8 + ((z + 1 - (i >> 4)) & 1) * 4 + ((split + offset) & 3)
         for src, dst, sem, arrived in ((code_ref, codes, code_sem, recv_code_sem), (row_ref, rows, row_sem, recv_sem)):
             pltpu.make_async_remote_copy(
                 src_ref=src.at[owner],
@@ -186,7 +191,7 @@
     @pl.when(is_direct)
     def _():
         fill_codes(chosen, label_ref[...], rank_ref[...], outgoing_code)
-        fill_rows(chosen, emb_ref[...], outgoing)
+        fill_rows(chosen, normalise(emb_ref[...]), outgoing)
         pl.semaphore_wait(barrier, jnp.where(is_home, N_SHARD - 1, jnp.where(low, N_SHARD, N_SHARD + 1)))
 
         def send_own(i, carry):
@@ -199,18 +204,22 @@
             pltpu.make_async_copy(outgoing_code.at[own], codes.at[own_place], recv_code_sem.at[group]).start()
             pltpu.make_async_copy(outgoing.at[own], rows.at[own_place], recv_sem.at[group]).start()
 
+        lax.fori_loop(0, N_SHARD - 1, send_own, 0)
+
         @pl.when(jnp.logical_not(is_home))
         def _():
-            send_own(0, 0)
-
-        lax.fori_loop(1, N_SHARD, send_own, 0)
+            send_own(N_SHARD - 1, 0)
 
     @pl.when(is_relay)
     def _():
-        for i in range(4):
+        for i in range(3):
             relay_copy(i).wait_recv()
         relay_chosen = slot_masks(relay_list[...])
         fill_codes(relay_chosen, relay_label[...], relay_rank[...], relay_outgoing_code)
+        for i in range(PIECES):
+            relay_copy(3 + i).wait_recv()
+            part = pl.ds(i * piece, piece)
+            relay_emb[part] = normalise(relay_emb[part])
         fill_rows(relay_chosen, relay_emb[...], relay_outgoing)
         place = place_of(y, 3 - z, core, split)
 
@@ -337,8 +346,8 @@
             pltpu.VMEM((DEVICES * CAP // LANES, 1, LANES), jnp.float32),
             pltpu.VMEM((N_SHARD, 1, LANES), jnp.float32),
             pltpu.SemaphoreType.DMA((4,)),
-            pltpu.SemaphoreType.DMA((4,)),
-            pltpu.SemaphoreType.DMA((4,)),
+            pltpu.SemaphoreType.DMA((3 + PIECES,)),
+            pltpu.SemaphoreType.DMA((3 + PIECES,)),
             pltpu.SemaphoreType.DMA,
             pltpu.SemaphoreType.DMA,
             pltpu.SemaphoreType.DMA,

time: 27.1 us -> 25.9 us (0.956)
  Pallas kernels: 26.4 us -> 25.2 us
    pallas_call x1, Pallas kernels: 26.4 us -> 25.2 us  [local(): pl.pallas_call(kernel, out_shape=jax.ShapeDtypeStruct((1, rows_dev), jnp....]
where the time goes in v3:
time: 25.9 us; the launch traced here: 25.8 us
  Pallas kernels  25.2 us (97%)
  local copies, waits for them, and re-layouts  0.51 us (2%)
    pallas_call x1, Pallas kernels, local(): pl.pallas_call(kernel, out_shape=jax.ShapeDtypeStruct((1, rows_dev), jnp....  25.2 us

profile of v3, /device:TPU:1, one launch (start us, length us, event | category | flops | bytes accessed | tf_op | source)
XLA Modules:
  0.0 25.8 jit_solution(12220677267076254407)
XLA Ops:
  0.0 25.2 %shard_map.46 = f32[1,128]{1,0:T(1,128)S(1)} custom-call(bf16[128,1024]{1,0:T(8,128)(2,1)} %emb_hbm.1, s32[1,128]{1,0:T(1,128)} %bitcast.8, s32[1,128]{1,0:T(1,128)} %bitcast.9, s32[8,32]{1,0:T(8,128)} %bitcast.7), custom_call_target="tpu_custom_call" | custom-call | tf_op jit(solution)/shard_map/pallas_call | solution.py:324
  25.2 0.5 %copy.6 = f32[128]{0:T(128)} copy(f32[128]{0:T(128)S(1)} %bitcast.6) | data formatting | bytes 1024

commit v4 on v3

--- a/solution.py
+++ b/solution.py
@@ -84,6 +84,8 @@
     codes,
     table,
     code_col,
+    first_col,
+    by_row,
     best,
     returned,
     in_sem,
@@ -238,10 +240,26 @@
         diagonal = iota((per_group, CAP, LANES), 1) == iota((per_group, CAP, LANES), 2)
         uppers, lowers, bests = [], [], []
 
-        def scored(scores, tile, col, query):
-            match = (col < uppers[query]) & (col >= lowers[query])
-            scores = scores[:, tile * LANES : (tile + 1) * LANES]
-            return jnp.max(jnp.where(match, scores, -1.0), axis=0, keepdims=True)
+        def give_back(kinds, start, stop):
+            def back(column, carry):
+                for kind in kinds:
+                    plane, at_core = KINDS[kind]
+                    copy = pltpu.make_async_remote_copy(
+                        src_ref=best.at[kind],
+                        dst_ref=returned.at[own],
+                        send_sem=back_send_sem,
+                        recv_sem=back_recv_sem,
+                        device_id=((column >> 2) * 8 + plane * 2 + at_core, column & 3),
+                        device_id_type=MESH,
+                    )
+                    if at_core == 1 and plane < 2:
+                        pl.when(kind * 16 + column != own_place)(copy.start)
+                    else:
+                        copy.start()
+                return carry
+
+            for column in range(start, stop):
+                back(column, 0)
 
         for g in range(GROUPS):
             part = pl.ds(g * per_group, per_group)
@@ -250,6 +268,7 @@
             col = jnp.sum(jnp.where(diagonal, codes[part], 0.0), axis=2, keepdims=True).reshape(size, 1)
             col = jnp.broadcast_to(col, (size, LANES))
             code_col[here] = col
+            first_col[here] = jnp.floor(col * (1.0 / RANK_SPAN)) * RANK_SPAN
             for t in range(tiles):
                 upper = jnp.sum(jnp.where(square, col[t * LANES : (t + 1) * LANES], 0.0), axis=0, keepdims=True)
                 uppers.append(upper)
@@ -258,40 +277,37 @@
             wait_bytes(rows.at[part], recv_sem.at[g])
             fresh = rows[part].reshape(size, width)
             table[here] = fresh
-            upto = (g + 1) * size
-            scores = lax.dot_general(table[:upto], fresh, contract, preferred_element_type=jnp.float32)
-            for t in range(tiles):
-                bests.append(scored(scores, t, code_col[:upto], g * tiles + t))
-            if g:
-                scores = lax.dot_general(fresh, table[: g * size], contract, preferred_element_type=jnp.float32)
-                for q in range(g * tiles):
-                    bests[q] = jnp.maximum(bests[q], scored(scores, q, col, q))
-        for q in range(GROUPS * tiles):
-            best[q] = bests[q]
-
+            found = [None] * tiles
+            for c in range(g + 1):
+                block = pl.ds(c * size, size)
+                scores = lax.dot_general(table[block], fresh, contract, preferred_element_type=jnp.float32)
+                newest = by_row[block] if c < g - 1 else None
+                for t in range(tiles):
+                    tile = scores[:, t * LANES : (t + 1) * LANES]
+                    upper, lower = uppers[g * tiles + t], lowers[g * tiles + t]
+                    match = (code_col[block] < upper) & (code_col[block] >= lower)
+                    value = jnp.max(jnp.where(match, tile, -1.0), axis=0, keepdims=True)
+                    found[t] = value if c == 0 else jnp.maximum(found[t], value)
+                    if c < g:
+                        match = (upper < code_col[block]) & (upper >= first_col[block])
+                        value = jnp.where(match, tile, -1.0)
+                        newest = value if newest is None else jnp.maximum(newest, value)
+                if c < g < GROUPS - 1:
+                    by_row[block] = newest
+                elif c < g:
+                    for t in range(tiles):
+                        kind = c * tiles + t
+                        value = jnp.max(newest[t * LANES : (t + 1) * LANES], axis=1, keepdims=True)
+                        value = jnp.max(jnp.where(square, value, -1.0), axis=0, keepdims=True)
+                        best[kind] = jnp.maximum(bests[kind], value)
+                    if c == 0:
+                        give_back((0, 1), 0, N_SPLIT)
+            bests += found
+        for kind in range((GROUPS - 1) * tiles, GROUPS * tiles):
+            best[kind] = bests[kind]
         pltpu.make_async_copy(best.at[own_place >> 4], returned.at[own], back_recv_sem).start()
-
-        def back(column, carry):
-            for kind, (plane, at_core) in enumerate(KINDS):
-                copy = pltpu.make_async_remote_copy(
-                    src_ref=best.at[kind],
-                    dst_ref=returned.at[own],
-                    send_sem=back_send_sem,
-                    recv_sem=back_recv_sem,
-                    device_id=((column >> 2) * 8 + plane * 2 + at_core, column & 3),
-                    device_id_type=MESH,
-                )
-                if at_core == 1 and plane < 2:
-
-                    @pl.when(kind * 16 + column != own_place)
-                    def _():
-                        copy.start()
-
-                else:
-                    copy.start()
-            return carry
-
-        lax.fori_loop(0, N_SHARD * N_SPLIT // len(KINDS), back, 0)
+        give_back(range(2, len(KINDS)), 0, N_SPLIT)
+        give_back(range(len(KINDS)), N_SPLIT, 16)
 
     lane = (y * 4 + split) * CAP + iota((N_SHARD, CAP, LANES), 1)
     there = iota((N_SHARD, CAP, LANES), 2) == lane
@@ -343,6 +359,8 @@
             pltpu.VMEM((DEVICES, 1, LANES), jnp.float32),
             pltpu.VMEM((DEVICES * CAP, width), jnp.bfloat16),
             pltpu.VMEM((DEVICES * CAP, LANES), jnp.float32),
+            pltpu.VMEM((DEVICES * CAP, LANES), jnp.float32),
+            pltpu.VMEM((DEVICES * CAP, LANES), jnp.float32),
             pltpu.VMEM((DEVICES * CAP // LANES, 1, LANES), jnp.float32),
             pltpu.VMEM((N_SHARD, 1, LANES), jnp.float32),
             pltpu.SemaphoreType.DMA((4,)),

time: 25.9 us -> 25.1 us (0.969)
  Pallas kernels: 25.2 us -> 24.5 us
    pallas_call x1, Pallas kernels: 25.2 us -> 24.5 us  [local(): pl.pallas_call(kernel, out_shape=jax.ShapeDtypeStruct((1, rows_dev), jnp....]
where the time goes in v4:
time: 25.1 us; the launch traced here: 25 us
  Pallas kernels  24.5 us (98%)
  local copies, waits for them, and re-layouts  0.51 us (2%)
    pallas_call x1, Pallas kernels, local(): pl.pallas_call(kernel, out_shape=jax.ShapeDtypeStruct((1, rows_dev), jnp....  24.5 us
    unnamed x1, local copies, waits for them, and re-layouts  0.51 us

profile of v4, /device:TPU:1, one launch (start us, length us, event | category | flops | bytes accessed | tf_op | source)
XLA Modules:
  0.0 25.0 jit_solution(10076333296835606265)
XLA Ops:
  0.0 24.5 %shard_map.46 = f32[1,128]{1,0:T(1,128)S(1)} custom-call(bf16[128,1024]{1,0:T(8,128)(2,1)} %emb_hbm.1, s32[1,128]{1,0:T(1,128)} %bitcast.8, s32[1,128]{1,0:T(1,128)} %bitcast.9, s32[8,32]{1,0:T(8,128)} %bitcast.7), custom_call_target="tpu_custom_call" | custom-call | tf_op jit(solution)/shard_map/pallas_call | solution.py:340
  24.5 0.5 %copy.6 = f32[128]{0:T(128)} copy(f32[128]{0:T(128)S(1)} %bitcast.6) | data formatting | bytes 1024

commit v5 on v4

--- a/solution.py
+++ b/solution.py
@@ -11,6 +11,7 @@
 CAP = 8
 GROUPS = 4
 PIECES = 4
+AHEAD = 3
 LANES = 128
 RANK_SPAN = 16384
 MESH = pl.DeviceIdType.MESH
@@ -123,11 +124,12 @@
     @pl.when(is_home)
     def _():
         def greet(i, carry):
-            column = (y * 4 + split + i) & 15
+            offset = (jnp.where(i < 8, 1479272810, 205723615) >> ((i & 7) * 4)) & 15
+            column = ((y + (offset >> 2)) & 3) * 4 + ((split + offset) & 3)
             for plane, at_core in ((0, 0), (1, 0), (0, 1), (1, 1), (2, 1), (3, 1)):
                 target = ((column >> 2) * 8 + plane * 2 + at_core, column & 3)
 
-                @pl.when(jnp.logical_or(i != 0, jnp.logical_or(z != plane, at_core == 0)))
+                @pl.when(jnp.logical_or(i != 15, jnp.logical_or(z != plane, at_core == 0)))
                 def _():
                     pl.semaphore_signal(barrier, inc=1, device_id=target, device_id_type=MESH)
 
@@ -167,7 +169,7 @@
 
     @pl.when(is_relayed)
     def _():
-        for i in range(3 + PIECES):
+        for i in range(3 + AHEAD):
             relay_copy(i).wait_send()
         pl.semaphore_signal(barrier, inc=1, device_id=(shard + 1, split), device_id_type=MESH)
 
@@ -332,6 +334,12 @@
         wait_bytes(relay_outgoing, relay_out_sem)
         wait_bytes(relay_outgoing_code, relay_out_code_sem)
 
+    @pl.when(is_relayed)
+    def _():
+        for i in range(3 + AHEAD, 3 + PIECES):
+            relay_copy(i).wait_send()
+
+
 def local(embeddings, order_rank, labels, send_list):
     rows_dev, width = embeddings.shape
     inputs = (embeddings, order_rank.reshape(1, rows_dev), labels.reshape(1, rows_dev), send_list[0].T)

time: 25.1 us -> 24.4 us (0.972)
  Pallas kernels: 24.5 us -> 23.8 us
    pallas_call x1, Pallas kernels: 24.5 us -> 23.8 us  [local(): pl.pallas_call(kernel, out_shape=jax.ShapeDtypeStruct((1, rows_dev), jnp....]
where the time goes in v5:
time: 24.4 us; the launch traced here: 24.3 us
  Pallas kernels  23.8 us (98%)
  local copies, waits for them, and re-layouts  0.51 us (2%)
    pallas_call x1, Pallas kernels, local(): pl.pallas_call(kernel, out_shape=jax.ShapeDtypeStruct((1, rows_dev), jnp....  23.8 us
    unnamed x1, local copies, waits for them, and re-layouts  0.51 us

profile of v5, /device:TPU:1, one launch (start us, length us, event | category | flops | bytes accessed | tf_op | source)
XLA Modules:
  0.0 24.3 jit_solution(17105110659823488795)
XLA Ops:
  0.0 23.8 %shard_map.46 = f32[1,128]{1,0:T(1,128)S(1)} custom-call(bf16[128,1024]{1,0:T(8,128)(2,1)} %emb_hbm.1, s32[1,128]{1,0:T(1,128)} %bitcast.8, s32[1,128]{1,0:T(1,128)} %bitcast.9, s32[8,32]{1,0:T(8,128)} %bitcast.7), custom_call_target="tpu_custom_call" | custom-call | tf_op jit(solution)/shard_map/pallas_call | solution.py:348
  23.8 0.5 %copy.6 = f32[128]{0:T(128)} copy(f32[128]{0:T(128)S(1)} %bitcast.6) | data formatting | bytes 1024

commit v6 on v5

--- a/solution.py
+++ b/solution.py
@@ -276,9 +276,24 @@
                 uppers.append(upper)
                 lowers.append(jnp.floor(upper * (1.0 / RANK_SPAN)) * RANK_SPAN)
 
+            last = g == GROUPS - 1
+            if last:
+                for t in range(tiles):
+                    value = jnp.max(by_row[t * LANES : (t + 1) * LANES], axis=1, keepdims=True)
+                    value = jnp.max(jnp.where(square, value, -1.0), axis=0, keepdims=True)
+                    bests[t] = jnp.maximum(bests[t], value)
+
             wait_bytes(rows.at[part], recv_sem.at[g])
             fresh = rows[part].reshape(size, width)
             table[here] = fresh
+            if last:
+                scores = lax.dot_general(fresh, table[:size], contract, preferred_element_type=jnp.float32)
+                for t in range(tiles):
+                    match = (col < uppers[t]) & (col >= lowers[t])
+                    value = jnp.where(match, scores[:, t * LANES : (t + 1) * LANES], -1.0)
+                    best[t] = jnp.maximum(bests[t], jnp.max(value, axis=0, keepdims=True))
+                give_back((0, 1), 0, N_SPLIT)
+
             found = [None] * tiles
             for c in range(g + 1):
                 block = pl.ds(c * size, size)
@@ -290,20 +305,18 @@
                     match = (code_col[block] < upper) & (code_col[block] >= lower)
                     value = jnp.max(jnp.where(match, tile, -1.0), axis=0, keepdims=True)
                     found[t] = value if c == 0 else jnp.maximum(found[t], value)
-                    if c < g:
+                    if c < g and not (last and c == 0):
                         match = (upper < code_col[block]) & (upper >= first_col[block])
                         value = jnp.where(match, tile, -1.0)
                         newest = value if newest is None else jnp.maximum(newest, value)
-                if c < g < GROUPS - 1:
+                if c < g and not last:
                     by_row[block] = newest
-                elif c < g:
+                elif 0 < c < g:
                     for t in range(tiles):
                         kind = c * tiles + t
                         value = jnp.max(newest[t * LANES : (t + 1) * LANES], axis=1, keepdims=True)
                         value = jnp.max(jnp.where(square, value, -1.0), axis=0, keepdims=True)
                         best[kind] = jnp.maximum(bests[kind], value)
-                    if c == 0:
-                        give_back((0, 1), 0, N_SPLIT)
             bests += found
         for kind in range((GROUPS - 1) * tiles, GROUPS * tiles):
             best[kind] = bests[kind]

time: 24.4 us -> 24.3 us (level)
  no operation moved by 1% of the time
where the time goes in v6:
time: 24.3 us; the launch traced here: 24.2 us
  Pallas kernels  23.7 us (98%)
  local copies, waits for them, and re-layouts  0.51 us (2%)
    pallas_call x1, Pallas kernels, local(): pl.pallas_call(kernel, out_shape=jax.ShapeDtypeStruct((1, rows_dev), jnp....  23.7 us
    unnamed x1, local copies, waits for them, and re-layouts  0.51 us

profile of v6, /device:TPU:1, one launch (start us, length us, event | category | flops | bytes accessed | tf_op | source)
XLA Modules:
  0.0 24.2 jit_solution(3619274124940161417)
XLA Ops:
  0.0 23.7 %shard_map.46 = f32[1,128]{1,0:T(1,128)S(1)} custom-call(bf16[128,1024]{1,0:T(8,128)(2,1)} %emb_hbm.1, s32[1,128]{1,0:T(1,128)} %bitcast.8, s32[1,128]{1,0:T(1,128)} %bitcast.9, s32[8,32]{1,0:T(8,128)} %bitcast.7), custom_call_target="tpu_custom_call" | custom-call | tf_op jit(solution)/shard_map/pallas_call | solution.py:361
  23.7 0.5 %copy.6 = f32[128]{0:T(128)} copy(f32[128]{0:T(128)S(1)} %bitcast.6) | data formatting | bytes 1024

commit v7 on v5

--- a/solution.py
+++ b/solution.py
@@ -10,6 +10,7 @@
 DEVICES = N_SHARD * N_SPLIT
 CAP = 8
 GROUPS = 4
+FAR = ((2, 2), (1, 2), (3, 2), (0, 2), (2, 1), (1, 1), (3, 1), (0, 1), (2, 3), (1, 3), (3, 3), (0, 3), (2, 0), (1, 0), (3, 0), (0, 0))
 PIECES = 4
 AHEAD = 3
 LANES = 128
@@ -123,19 +124,17 @@
 
     @pl.when(is_home)
     def _():
-        def greet(i, carry):
-            offset = (jnp.where(i < 8, 1479272810, 205723615) >> ((i & 7) * 4)) & 15
-            column = ((y + (offset >> 2)) & 3) * 4 + ((split + offset) & 3)
+        for dx, dy in FAR:
+            base, x = ((y + dy) & 3) * 8, (split + dx) & 3
             for plane, at_core in ((0, 0), (1, 0), (0, 1), (1, 1), (2, 1), (3, 1)):
-                target = ((column >> 2) * 8 + plane * 2 + at_core, column & 3)
-
-                @pl.when(jnp.logical_or(i != 15, jnp.logical_or(z != plane, at_core == 0)))
-                def _():
-                    pl.semaphore_signal(barrier, inc=1, device_id=target, device_id_type=MESH)
-
-            return carry
-
-        lax.fori_loop(0, 16, greet, 0)
+
+                def greet():
+                    pl.semaphore_signal(barrier, inc=1, device_id=(base + plane * 2 + at_core, x), device_id_type=MESH)
+
+                if dx == dy == 0 and at_core == 1 and plane < 2:
+                    pl.when(z != plane)(greet)
+                else:
+                    greet()
 
     inputs = (list_hbm, rank_hbm, label_hbm, emb_hbm)
     piece = emb_ref.shape[0] // PIECES
@@ -180,7 +179,7 @@
 
     def send(i, place, code_ref, code_sem, row_ref, row_sem):
         k = i & 15
-        offset = (jnp.where(k < 8, 1479272810, 205723615) >> ((k & 7) * 4)) & 15
+        offset = (jnp.where(k < 8, 1196854170, 51564510) >> ((k & 7) * 4)) & 15
         owner = ((y + (offset >> 2)) & 3) * 8 + ((z + 1 - (i >> 4)) & 1) * 4 + ((split + offset) & 3)
         for src, dst, sem, arrived in ((code_ref, codes, code_sem, recv_code_sem), (row_ref, rows, row_sem, recv_sem)):
             pltpu.make_async_remote_copy(

time: 24.4 us -> 24.4 us (level)
  no operation moved by 1% of the time
where the time goes in v7:
time: 24.4 us; the launch traced here: 24.3 us
  Pallas kernels  23.7 us (97%)
  local copies, waits for them, and re-layouts  0.51 us (2%)
    pallas_call x1, Pallas kernels, local(): pl.pallas_call(kernel, out_shape=jax.ShapeDtypeStruct((1, rows_dev), jnp....  23.7 us
    unnamed x1, local copies, waits for them, and re-layouts  0.51 us

profile of v7, /device:TPU:1, one launch (start us, length us, event | category | flops | bytes accessed | tf_op | source)
XLA Modules:
  0.0 24.3 jit_solution(13727370750621962675)
XLA Ops:
  0.0 23.7 %shard_map.46 = f32[1,128]{1,0:T(1,128)S(1)} custom-call(bf16[128,1024]{1,0:T(8,128)(2,1)} %emb_hbm.1, s32[1,128]{1,0:T(1,128)} %bitcast.8, s32[1,128]{1,0:T(1,128)} %bitcast.9, s32[8,32]{1,0:T(8,128)} %bitcast.7), custom_call_target="tpu_custom_call" | custom-call | tf_op jit(solution)/shard_map/pallas_call | solution.py:347
  23.8 0.5 %copy.6 = f32[128]{0:T(128)} copy(f32[128]{0:T(128)S(1)} %bitcast.6) | data formatting | bytes 1024

commit v8 on v5

--- a/solution.py
+++ b/solution.py
@@ -59,8 +59,11 @@
 
 
 def fill_rows(chosen, normed, outgoing):
-    picked = jnp.dot(chosen.astype(jnp.bfloat16), normed, preferred_element_type=jnp.float32)
-    outgoing[...] = picked.astype(jnp.bfloat16).reshape(outgoing.shape)
+    onehot = chosen.astype(jnp.bfloat16)
+    for start in range(0, normed.shape[1], 256):
+        part = slice(start, start + 256)
+        picked = jnp.dot(onehot, normed[:, part], preferred_element_type=jnp.float32)
+        outgoing[:, :, part] = picked.astype(jnp.bfloat16).reshape(N_SHARD, CAP, 256)
 
 
 def kernel(

time: 24.4 us -> 24.4 us (level)
  no operation moved by 1% of the time
where the time goes in v8:
time: 24.4 us; the launch traced here: 24.3 us
  Pallas kernels  23.8 us (98%)
  local copies, waits for them, and re-layouts  0.51 us (2%)
    pallas_call x1, Pallas kernels, local(): pl.pallas_call(kernel, out_shape=jax.ShapeDtypeStruct((1, rows_dev), jnp....  23.8 us
    unnamed x1, local copies, waits for them, and re-layouts  0.51 us

profile of v8, /device:TPU:1, one launch (start us, length us, event | category | flops | bytes accessed | tf_op | source)
XLA Modules:
  0.0 24.3 jit_solution(17105110659823488795)
XLA Ops:
  0.0 23.8 %shard_map.46 = f32[1,128]{1,0:T(1,128)S(1)} custom-call(bf16[128,1024]{1,0:T(8,128)(2,1)} %emb_hbm.1, s32[1,128]{1,0:T(1,128)} %bitcast.8, s32[1,128]{1,0:T(1,128)} %bitcast.9, s32[8,32]{1,0:T(8,128)} %bitcast.7), custom_call_target="tpu_custom_call" | custom-call | tf_op jit(solution)/shard_map/pallas_call | solution.py:351
  23.8 0.5 %copy.6 = f32[128]{0:T(128)} copy(f32[128]{0:T(128)S(1)} %bitcast.6) | data formatting | bytes 1024
